TPU v7x, 32 devices: a whole 2x2x4 slice. The times are simulated.
32 devices in a mesh: row: 16 (over z, y, x), col: 2 (over core).
Axes of the slice: x: 2, y: 2, z: 4, core: 2. Of those that a mesh axis runs over, the one named last changes fastest.
Arguments:
- features: bfloat16 [128, 4096], P('col', 'row'), may hold values from -6 to 6
- order: int32 [4096], P('row'), may hold values from 0 to 4095, as said below
- weight: bfloat16 [128, 256], P(None, 'col'), may hold values from -0.5 to 0.5
- bias: bfloat16 [256], P('col'), may hold values from -3 to 3
- tiles: bfloat16 [32, 64, 128, 128], P('row'), may hold values from -0.09375 to 0.09375
- coords: int32 [32, 64], P('row'), may hold values from 0 to 31
- counts: int32 [32], P('row'), may hold values from 1 to 64, 1024 in all
- grad_hidden: bfloat16 [256, 4096], P('col', 'row'), may hold values from -6 to 6
Outputs:
- hidden: bfloat16 [256, 4096], P('col', 'row')
- grad_features: float32 [128, 4096], P('col', 'row')
- grad_weight: float32 [128, 256], P(None, 'col')
- grad_bias: float32 [256], P('col')
Inputs may be any that keep to these rules, and one draw needn't show every extreme that they name: Within each aligned block of 256 nodes, order is a permutation of that block's node indices. `counts`: some block row fills all 64 slots. `coords`: slots of one block row may name the same column block.
All inputs are finite; a program needn't handle non-finite values.
Results may differ from a plain program's by a relative error of at most 0.0015.
Values may be sent and summed in bfloat16 or wider, within the bound.
A program may use at most 64 MiB of HBM per device.

v0:
```python
import math

import jax
import jax.numpy as jnp
from jax import lax
from jax.sharding import PartitionSpec as P


def aggregate(source, tiles, flat_coords, flat_live):
    feature_count = source.shape[0]
    blocks_here, slot_count, tile_size = (tiles.shape[0], tiles.shape[1], tiles.shape[2])
    shaped = source.reshape(feature_count, -1, tile_size)
    picked = jnp.take(shaped, flat_coords, axis=1)
    picked = picked * flat_live.reshape(1, -1, 1).astype(picked.dtype)
    picked = picked.reshape(feature_count, blocks_here, slot_count, tile_size)
    result = jnp.einsum(
        "fikc,ikrc->fir", picked, tiles.astype(jnp.float32), precision=lax.Precision.HIGHEST
    )
    return result.reshape(feature_count, blocks_here * tile_size)


def slot_terms(grad_rows, tiles, flat_live):
    feature_count = grad_rows.shape[0]
    blocks_here, slot_count, tile_size = (tiles.shape[0], tiles.shape[1], tiles.shape[2])
    grad_blocks = grad_rows.reshape(feature_count, blocks_here, tile_size)
    contrib = jnp.einsum(
        "fir,ikrc->ikfc", grad_blocks, tiles.astype(jnp.float32), precision=lax.Precision.HIGHEST
    )
    contrib = contrib.reshape(blocks_here * slot_count, feature_count * tile_size)
    return contrib * flat_live.astype(jnp.float32)[:, None]


def make_picker(contrib, flat_coords, count):
    targets = lax.broadcasted_iota(jnp.int32, (count, 1), 0)
    onehot = (flat_coords[None, :] == targets).astype(jnp.float32)
    return jnp.dot(onehot, contrib, precision=lax.Precision.HIGHEST)


def unpack_rows(summed_rows, feature_count, tile_size):
    blocks_here = summed_rows.shape[0]
    shaped = summed_rows.reshape(blocks_here, feature_count, tile_size)
    return jnp.transpose(shaped, (1, 0, 2)).reshape(feature_count, blocks_here * tile_size)


def per_device(features, order, weight, bias, tiles, coords, counts, grad_hidden):
    rows_here = order.shape[0]
    tile_size = tiles.shape[2]
    local_index = order - lax.axis_index("row") * rows_here
    reordered = jnp.take(features, local_index, axis=1)
    blocks_here, slot_count = coords.shape
    slot_live = lax.broadcasted_iota(jnp.int32, (blocks_here, slot_count), 1) < counts[:, None]
    flat_coords = coords.reshape(-1)
    flat_live = slot_live.reshape(-1)
    weight_wide = weight.astype(jnp.float32)
    norm_factor = 1.0 / math.sqrt(rows_here * lax.axis_size("row"))
    bias_column = bias.astype(jnp.float32)[:, None]
    every_feature = lax.all_gather(reordered, "col", axis=0, tiled=True)
    projected = jnp.dot(weight.T, every_feature, preferred_element_type=jnp.float32)
    all_projected = lax.all_gather(projected, "row", axis=1, tiled=True)
    pre_act = aggregate(all_projected, tiles, flat_coords, flat_live) + bias_column
    gate_value = jax.nn.sigmoid(pre_act)
    hidden = (pre_act * gate_value).astype(jnp.bfloat16)
    grad_pre = grad_hidden.astype(jnp.float32) * gate_value * (1.0 + pre_act * (1.0 - gate_value))
    contrib = slot_terms(grad_pre, tiles, flat_live)
    summed_rows = lax.psum_scatter(
        make_picker(contrib, flat_coords, blocks_here * lax.axis_size("row")),
        "row",
        scatter_dimension=0,
        tiled=True,
    )
    column_grad = unpack_rows(summed_rows, grad_pre.shape[0], tile_size)
    feature_terms = jnp.dot(weight_wide, column_grad, precision=lax.Precision.HIGHEST)
    grad_features = lax.psum_scatter(feature_terms, "col", scatter_dimension=0, tiled=True)
    left_side = every_feature.astype(jnp.float32)
    weight_part = jnp.dot(left_side, column_grad.T, precision=lax.Precision.HIGHEST)
    bias_part = jnp.sum(grad_pre, axis=1)
    grad_weight, grad_bias = lax.psum((weight_part, bias_part), "row")
    return (hidden, grad_features, grad_weight * norm_factor, grad_bias * norm_factor)


def solution(mesh):
    in_specs = (
        P("col", "row"),
        P("row"),
        P(None, "col"),
        P("col"),
        P("row", None, None, None),
        P("row", None),
        P("row"),
        P("col", "row"),
    )
    out_specs = (P("col", "row"), P("col", "row"), P(None, "col"), P("col"))
    return jax.shard_map(
        per_device, mesh=mesh, in_specs=in_specs, out_specs=out_specs, check_vma=False
    )
```

profile of v0, /device:TPU:0, one launch (start us, length us, event | category | flops | bytes accessed | tf_op | source)
XLA Modules:
  0.0 365.3 jit_solution(6250998067234618678)
XLA Ops:
  7.2 0.7 compare_and_fusion
  7.9 0.9 copy.29
  8.8 0.9 gather_fusion
  9.7 0.1 select_bitcast_fusion
  9.8 0.1 copy.30
  9.9 2.0 all_gather.6
  11.8 0.8 convolution_bitcast_fusion.1
  12.7 0.8 reshape.107
  13.5 0.8 reshape.109
  14.3 0.7 convert_element_type.33
  14.9 0.8 compare_convert_fusion
  15.7 0.1 reshape.114
  15.8 60.4 %all-gather.2.cloned.1.call-done = f32[128,4096]{0,1:T(8,128)} async-done(((f32[128,256]{0,1:T(8,128)}), f32[128,4096]{0,1:T(8,128)}) %all-gather.2.cloned.1.call-update) | async-done | bytes 2097168 | tf_op jit(solution)/shard_map/all_gather | solution.py:59
  76.1 5.9 %gather_fusion.1 = f32[128,128,128]{1,2,0:T(8,128)} fusion(f32[128,32,128]{0,2,1:T(8,128)} %bitcast.43, s32[1024]{0:T(1024)S(1)} %pad_clamp_fusion), kind=kCustom, calls=%fused_computation.1 | custom fusion | bytes 16777728 | tf_op jit(solution)/shard_map/jit(_take)/gather | solution.py:13
  82.0 9.0 %copy.31 = f32[128,128,128]{2,0,1:T(8,128)} copy(f32[128,128,128]{0,2,1:T(8,128)} %bitcast.44) | data formatting | bytes 16777216 | tf_op jit(solution)/shard_map/jit(_take)/gather | solution.py:13
  91.0 9.7 %fusion.2 = f32[2,128,128,1]{1,2,3,0:T(8,128)S(1)} fusion(bf16[2,64,128,128]{3,2,1,0:T(8,128)(2,1)} %param.12, f32[128,2,64,128]{3,0,2,1:T(8,128)} %bitcast.45, f32[2,64]{1,0:T(2,128)S(1)} %get-tuple-element.25, pred[2,64]{1,0:T(4,128)(4,1)S(1)} %get-tuple-element.26), kind=kOutput, calls=%fused_computation.5 | convolution fusion | flops 3225419776 | bytes 12714624 | tf_op jit(solution)/shard_map/fikc,ikrc->fir/dot_general | solution.py:16
  100.7 0.1 copy.32
  100.8 0.8 fusion.14
  101.7 5.4 %fusion.9 = f32[2,128,64,128]{3,1,2,0:T(8,128)S(1)} fusion(bf16[2,64,128,128]{3,2,1,0:T(8,128)(2,1)} %param.12, f32[128,2,128,1]{2,1,0,3:T(2,128)S(1)} %bitcast.50), kind=kOutput, calls=%fused_computation.16 | convolution fusion | flops 3221225472 | bytes 12713984 | tf_op jit(solution)/shard_map/fir,ikrc->ikfc/dot_general | solution.py:26
  107.1 8.9 %fusion = f32[32,16384]{1,0:T(8,128)} fusion(f32[16,8,128,128]{3,2,1,0:T(8,128)S(1)} %bitcast.46, f32[128]{0:T(128)S(1)} %reshape.114, s32[128]{0:T(128)S(1)} %reshape.109), kind=kOutput, calls=%fused_computation.3 | convolution fusion | flops 807407616 | bytes 10486784 | tf_op jit(solution)/shard_map/dot_general | solution.py:36
  116.1 0.6 dynamic-slice
  117.3 40.4 %psum.15 = f32[128]{0:T(128)S(1)} all-reduce(f32[128]{0:T(128)S(1)} %get-tuple-element.20), channel_id=1, replica_groups=mesh['row'=16,'col'=2] {'row'}, use_global_device_ids=true, to_apply=%region_4.5 | all-reduce | flops 128 | bytes 1024 | tf_op jit(solution)/shard_map/psum | solution.py:77
  157.7 83.5 %all-reduce.6.cloned.1.call-done = f32[32,16384]{1,0:T(8,128)} async-done(((f32[32,16384]{1,0:T(8,128)}), f32[32,16384]{1,0:T(8,128)}) %all-reduce.6.cloned.1.call-update) | async-done | bytes 2097168
  241.2 1.1 dynamic-slice_bitcast_fusion
  242.3 0.1 copy.34
  242.4 0.8 fusion.15
  243.3 0.2 convolution_bitcast_fusion
  243.6 0.7 copy.40
  244.3 0.5 broadcast_multiply_fusion.1
  244.9 104.7 %all-reduce.4.cloned.1.call-done = f32[128,128]{1,0:T(8,128)} async-done(((f32[128,128]{1,0:T(8,128)}), f32[128,128]{1,0:T(8,128)}) %all-reduce.4.cloned.1.call-update) | async-done | bytes 65552 | tf_op jit(solution)/shard_map/psum | solution.py:77
  349.6 1.5 broadcast_multiply_fusion
  351.0 7.7 %reduce-scatter.4.cloned.1.call-done = f32[64,256]{1,0:T(8,128)} async-done(((f32[128,256]{1,0:T(8,128)}), f32[64,256]{1,0:T(8,128)}) %reduce-scatter.4.cloned.1.call-update) | async-done | bytes 65552
  (19 shorter events, 0.3 us)
Async XLA Ops:
  7.2 4.7 %copy-start = (bf16[128,128]{1,0:T(8,128)(2,1)S(1)}, bf16[128,128]{1,0:T(8,128)(2,1)}, u32[]{:S(2)}) copy-start(bf16[128,128]{1,0:T(8,128)(2,1)} %param.10) | copy-start | bytes 98308
  7.2 69.0 %all-gather.2.cloned.1.call-start = ((), (), s32[]{:S(2)}) async-start(), calls=%async_computation.1 | async-start | bytes 2228224 | tf_op jit(solution)/shard_map/all_gather | solution.py:59
  12.7 228.5 %all-reduce.6.cloned.1.call-start = ((), (), s32[]{:S(2)}) async-start(), calls=%async_computation.4 | async-start | bytes 4194304
  91.0 9.8 %copy-start.1 = (bf16[128,256]{1,0:T(8,128)(2,1)S(1)}, bf16[128,256]{1,0:T(8,128)(2,1)}, u32[]{:S(2)}) copy-start(bf16[128,256]{1,0:T(8,128)(2,1)} %param.15) | copy-start | bytes 196612
  107.0 9.0 %copy-start.2 = (u32[32]{0:T(128)S(1)}, u32[32]{0:T(128)}, u32[]{:S(2)}) copy-start(u32[32]{0:T(128)} %constant.50) | copy-start | bytes 388
  116.0 233.6 %all-reduce.4.cloned.1.call-start = ((), (), s32[]{:S(2)}) async-start(), calls=%async_computation.2 | async-start | bytes 131072 | tf_op jit(solution)/shard_map/psum | solution.py:77
  243.3 115.5 %reduce-scatter.4.cloned.1.call-start = ((), (), s32[]{:S(2)}) async-start(), calls=%async_computation.3 | async-start | bytes 196608
Sparse Core Ops, SparseCore 0:
  12.8 63.2 all-gather.1
  116.1 125.0 all-reduce.5
  248.2 101.3 all-reduce.3
  352.2 6.5 reduce-scatter.3
where the time goes:
time: 366 us; the launch traced here: 365 us
  waiting for transfers between devices  256 us (70%)
  blocking collectives  42.4 us (12%)
  matrix products  25.9 us (7%)
  local copies, waits for them, and re-layouts  21 us (6%)
  between operations  14.5 us (4%)
  other arithmetic  4.98 us (1%)
    psum x1, waiting for transfers between devices, per_device(): grad_weight, grad_bias = lax.psum((weight_part, bias_part), 'row')  105 us
    unnamed x6, waiting for transfers between devices  91.3 us
    all_gather x1, waiting for transfers between devices, per_device(): all_projected = lax.all_gather(projected, 'row', axis=1, tiled=True)  60.4 us
    psum x1, blocking collectives, per_device(): grad_weight, grad_bias = lax.psum((weight_part, bias_part), 'row')  40.4 us
    gather x2, local copies, waits for them, and re-layouts, aggregate(): picked = jnp.take(shaped, flat_coords, axis=1)  14.9 us
    dot_general x1, matrix products, aggregate(): jnp.einsum('fikc,ikrc->fir', picked, tiles.astype(jnp.float32), precision...  9.68 us
    dot_general x1, matrix products, make_picker(): return jnp.dot(onehot, contrib, precision=lax.Precision.HIGHEST)  8.94 us
  transfers between devices with their start and end apart: 4, of which 4 were waited for; matrix products, arithmetic and copies ran while one was open for 2% of the time, Pallas kernels for 0%

commit v1 on v0

v1 whole, which is shorter than its diff:
```python
import functools
import math

import jax
import jax.numpy as jnp
from jax import lax
from jax.experimental import pallas as pl
from jax.experimental.pallas import tpu as pltpu
from jax.sharding import PartitionSpec as P

MESH = pl.DeviceIdType.MESH
F32 = jnp.float32
BF16 = jnp.bfloat16
GROUP = 8
VMEM_LIMIT = 56 * 1024 * 1024

NN = (((1,), (0,)), ((), ()))
NT = (((1,), (1,)), ((), ()))
TN = (((0,), (0,)), ((), ()))


def mm(a, b, dims):
    return lax.dot_general(a, b, dims, preferred_element_type=F32)


def split(x):
    hi = x.astype(BF16)
    return hi, (x - hi.astype(F32)).astype(BF16)


def build_kernel(tiles, coords, counts, hi_ref, lo_ref, buf, acc, sems):
    rows, slots, tile, _ = buf.shape
    groups = slots // GROUP

    def copy(i, g):
        part = pl.ds(g * GROUP, GROUP)
        return pltpu.make_async_copy(tiles.at[i, part], buf.at[i, part], sems.at[i, g])

    for g in range(groups):
        for i in range(rows):
            @pl.when(counts[i] > g * GROUP)
            def _():
                copy(i, g).start()
    acc[...] = jnp.zeros_like(acc)
    for g in range(groups):
        for i in range(rows):
            live = jnp.clip(counts[i] - g * GROUP, 0, GROUP)

            @pl.when(live > 0)
            def _():
                copy(i, g).wait()

                def add(k, carry):
                    at = g * GROUP + k
                    j = coords[i, at]
                    mine = pl.ds(i * tile, tile)
                    acc[j, mine, :] = acc[j, mine, :] + buf[i, at].astype(F32)
                    return carry

                lax.fori_loop(0, live, add, 0)
    pieces = hi_ref.shape[0]

    def convert(p, carry):
        for h in range(rows):
            hi, lo = split(acc[p * rows + h])
            hi_ref[p, :, h * tile:(h + 1) * tile] = hi
            lo_ref[p, :, h * tile:(h + 1) * tile] = lo
        return carry

    lax.fori_loop(0, pieces, convert, 0)


def layer_kernel(
    rz, rp, cn, norm,
    order, feat, weight, bias, grad_hidden, hi_any, lo_any,
    hid_out, gf_out, gw_out, gb_out,
    ahi, alo, xall, yfull, zpart, zrecv, c1send, c1recv, c2send, c2recv,
    g1send, g1recv, g2send, g2recv, gall,
    a_sem, x_ss, x_rs, y_ss, y_rs, z_ss, z_rs, c1_ss, c1_rs, c2_ss, c2_rs,
    g1_ss, g1_rs, g2_ss, g2_rs, g3_ss, g3_rs,
):
    row, col = lax.axis_index("row"), lax.axis_index("col")
    zi, pi = row // rp, lax.rem(row, rp)
    fl, nodes = feat.shape
    hl = weight.shape[1]
    fin = weight.shape[0]
    fr = fin // rp

    def zmate(d):
        return (lax.rem(zi + d, rz) * rp + pi, col)

    def pmate(d):
        return (zi * rp + lax.rem(pi + d, rp), col)

    def cmate(d):
        return (row, lax.rem(col + d, cn))

    mates = [zmate(d) for d in range(1, rz)]
    mates += [pmate(d) for d in range(1, rp)]
    mates += [cmate(d) for d in range(1, cn)]

    def remote(src, dst, ss, rs, to):
        return pltpu.make_async_remote_copy(
            src_ref=src, dst_ref=dst, send_sem=ss, recv_sem=rs,
            device_id=to, device_id_type=MESH,
        )

    load_hi = pltpu.make_async_copy(hi_any, ahi, a_sem.at[0])
    load_lo = pltpu.make_async_copy(lo_any, alo, a_sem.at[1])
    load_hi.start()
    load_lo.start()
    barrier = pltpu.get_barrier_semaphore()
    for mate in mates:
        pl.semaphore_signal(barrier, inc=1, device_id=mate, device_id_type=MESH)

    local = order[...] - row * nodes
    pick = (lax.broadcasted_iota(jnp.int32, (nodes, nodes), 0) == local).astype(F32).astype(BF16)
    xall[0, 0] = mm(feat[...], pick, NN).astype(BF16)
    pl.semaphore_wait(barrier, len(mates))

    sent = []

    def go(c):
        c.start()
        sent.append(c)
        return c

    xz = {d: go(remote(xall.at[0, 0], xall.at[d, 0], x_ss.at[d, 0], x_rs.at[d, 0], zmate(d)))
          for d in range(1, rz)}
    xp = {}

    def relay(dz):
        for dp in range(1, rp):
            xp[dz, dp] = go(remote(xall.at[dz, 0], xall.at[dz, dp], x_ss.at[dz, dp],
                                   x_rs.at[dz, dp], pmate(dp)))

    relay(0)
    load_hi.wait()
    load_lo.wait()

    def piece(dz, dp):
        return lax.rem(zi + rz - dz, rz) * rp + lax.rem(pi + rp - dp, rp)

    def term(dz, dp):
        at = piece(dz, dp)
        x = xall[dz, dp]
        return mm(x, ahi[at], NT) + mm(x, alo[at], NT)

    y = term(0, 0)
    for dz in range(1, rz):
        xz[dz].wait_recv()
        relay(dz)
        y = y + term(dz, 0)
    for dz in range(rz):
        for dp in range(1, rp):
            xp[dz, dp].wait_recv()
            y = y + term(dz, dp)

    mine = pl.ds(pl.multiple_of(col * fl, fl), fl)
    yfull[mine, :] = y
    yx = [go(remote(yfull.at[mine], yfull.at[mine], y_ss.at[d], y_rs.at[d], cmate(d)))
          for d in range(1, cn)]
    for c in yx:
        c.wait_recv()
    y_hi, y_lo = split(yfull[...])

    w = weight[...]
    first = lax.broadcasted_iota(jnp.int32, (16, hl), 0) == 0
    bias_rows = jnp.where(first, bias[...].astype(F32), 0.0).astype(BF16)
    pre = mm(w, y_hi, TN) + mm(w, y_lo, TN) + mm(bias_rows, jnp.ones((16, nodes), BF16), TN)
    gate = jax.nn.sigmoid(pre)
    hid_out[...] = (pre * gate).astype(BF16)
    grad_pre = grad_hidden[...].astype(F32) * gate * (1.0 + pre * (1.0 - gate))
    gp_hi, gp_lo = split(grad_pre)

    zpart[...] = mm(w, gp_hi, NN) + mm(w, gp_lo, NN)
    zx = []
    for d in range(1, cn):
        theirs = pl.ds(pl.multiple_of(lax.rem(col + d, cn) * fl, fl), fl)
        zx.append(go(remote(zpart.at[theirs], zrecv.at[d], z_ss.at[d], z_rs.at[d], cmate(d))))

    gw = mm(y_hi, gp_hi, NT) + mm(y_lo, gp_hi, NT) + mm(y_hi, gp_lo, NT)
    ones = jnp.ones((16, nodes), BF16)
    gb = (mm(ones, gp_hi, NT) + mm(ones, gp_lo, NT))[:8]
    for q in range(rp):
        g1send[q, :fr] = gw[q * fr:(q + 1) * fr]
        g1send[q, fr:] = gb
    g1 = [go(remote(g1send.at[lax.rem(pi + d, rp)], g1recv.at[d], g1_ss.at[d], g1_rs.at[d],
                    pmate(d))) for d in range(1, rp)]

    z = zpart[mine, :]
    for d in range(1, cn):
        zx[d - 1].wait_recv()
        z = z + zrecv[d]
    z_hi, z_lo = split(z)
    z_two = jnp.concatenate([z_hi, z_lo], axis=0)

    c1 = {}

    def contribute(d):
        for dp in list(range(1, rp)) + [0]:
            at = lax.rem(zi + d, rz) * rp + lax.rem(pi + dp, rp)
            both = mm(z_two, ahi[at], NN)
            c1send[d, dp] = both[:fl] + both[fl:] + mm(z_hi, alo[at], NN)
            if dp:
                c1[d, dp] = go(remote(c1send.at[d, dp], c1recv.at[d, dp], c1_ss.at[d, dp],
                                      c1_rs.at[d, dp], pmate(dp)))

    def reduced(d):
        total = c1send[d, 0]
        for dp in range(1, rp):
            c1[d, dp].wait_recv()
            total = total + c1recv[d, dp]
        return total

    c2 = {}

    def pass_on(d):
        c2send[d] = reduced(d)
        c2[d] = go(remote(c2send.at[d], c2recv.at[d], c2_ss.at[d], c2_rs.at[d], zmate(d)))

    contribute(1)
    for d in range(2, rz):
        contribute(d)
        pass_on(d - 1)
    contribute(0)
    pass_on(rz - 1)

    part = g1send[pi]
    for d in range(1, rp):
        g1[d - 1].wait_recv()
        part = part + g1recv[d]
    g2send[...] = part
    g2 = [go(remote(g2send, g2recv.at[d], g2_ss.at[d], g2_rs.at[d], zmate(d)))
          for d in range(1, rz)]
    total = reduced(0)
    for d in range(1, rz):
        g2[d - 1].wait_recv()
        part = part + g2recv[d]
    gall[pi] = part[:fr]
    g3 = [go(remote(gall.at[pi], gall.at[pi], g3_ss.at[d], g3_rs.at[d], pmate(d)))
          for d in range(1, rp)]
    gb_out[...] = part[fr:fr + 1] * norm
    for d in range(1, rz):
        c2[d].wait_recv()
        total = total + c2recv[d]
    gf_out[...] = total
    for c in g3:
        c.wait_recv()
    gw_out[...] = gall[...].reshape(fin, hl) * norm
    for c in sent:
        c.wait_send()


def per_device(r, cn, features, order, weight, bias, tiles, coords, counts, grad_hidden):
    rows, slots, tile, _ = tiles.shape
    nodes = order.shape[0]
    fl = features.shape[0]
    fin, hl = weight.shape
    rz = 4 if r % 4 == 0 else 1
    rp = r // rz
    fr = fin // rp
    norm = 1.0 / math.sqrt(nodes * r)
    vmem = pl.BlockSpec(memory_space=pltpu.VMEM)
    smem = pl.BlockSpec(memory_space=pltpu.SMEM)
    anyw = pl.BlockSpec(memory_space=pl.ANY)
    dense = jax.ShapeDtypeStruct((r, nodes, nodes), BF16)
    hi, lo = pl.pallas_call(
        build_kernel,
        out_shape=(dense, dense),
        in_specs=[anyw, smem, smem],
        out_specs=(vmem, vmem),
        scratch_shapes=[
            pltpu.VMEM((rows, slots, tile, tile), BF16),
            pltpu.VMEM((r * rows, nodes, tile), F32),
            pltpu.SemaphoreType.DMA((rows, slots // GROUP)),
        ],
        compiler_params=pltpu.CompilerParams(vmem_limit_bytes=VMEM_LIMIT),
        name="build_dense",
    )(tiles, coords, counts)

    dma = pltpu.SemaphoreType.DMA
    outs = (
        jax.ShapeDtypeStruct((hl, nodes), BF16),
        jax.ShapeDtypeStruct((fl, nodes), F32),
        jax.ShapeDtypeStruct((fin, hl), F32),
        jax.ShapeDtypeStruct((1, hl), F32),
    )
    hidden, gf, gw, gb = pl.pallas_call(
        functools.partial(layer_kernel, rz, rp, cn, norm),
        out_shape=outs,
        in_specs=[vmem] * 5 + [anyw] * 2,
        out_specs=(vmem,) * 4,
        scratch_shapes=[
            pltpu.VMEM((r, nodes, nodes), BF16),
            pltpu.VMEM((r, nodes, nodes), BF16),
            pltpu.VMEM((rz, rp, fl, nodes), BF16),
            pltpu.VMEM((fin, nodes), F32),
            pltpu.VMEM((fin, nodes), F32),
            pltpu.VMEM((cn, fl, nodes), F32),
            pltpu.VMEM((rz, rp, fl, nodes), F32),
            pltpu.VMEM((rz, rp, fl, nodes), F32),
            pltpu.VMEM((rz, fl, nodes), F32),
            pltpu.VMEM((rz, fl, nodes), F32),
            pltpu.VMEM((rp, fr + 8, hl), F32),
            pltpu.VMEM((rp, fr + 8, hl), F32),
            pltpu.VMEM((fr + 8, hl), F32),
            pltpu.VMEM((rz, fr + 8, hl), F32),
            pltpu.VMEM((rp, fr, hl), F32),
            dma((2,)),
            dma((rz, rp)), dma((rz, rp)),
            dma((cn,)), dma((cn,)),
            dma((cn,)), dma((cn,)),
            dma((rz, rp)), dma((rz, rp)),
            dma((rz,)), dma((rz,)),
            dma((rp,)), dma((rp,)),
            dma((rz,)), dma((rz,)),
            dma((rp,)), dma((rp,)),
        ],
        compiler_params=pltpu.CompilerParams(
            collective_id=0, has_side_effects=True, vmem_limit_bytes=VMEM_LIMIT
        ),
        name="layer",
    )(order.reshape(1, nodes), features, weight, bias.reshape(1, hl), grad_hidden, hi, lo)
    return hidden, gf, gw, gb.reshape(hl)


def solution(mesh):
    in_specs = (
        P("col", "row"),
        P("row"),
        P(None, "col"),
        P("col"),
        P("row", None, None, None),
        P("row", None),
        P("row"),
        P("col", "row"),
    )
    out_specs = (P("col", "row"), P("col", "row"), P(None, "col"), P("col"))
    return jax.shard_map(
        functools.partial(per_device, mesh.shape["row"], mesh.shape["col"]),
        mesh=mesh, in_specs=in_specs, out_specs=out_specs, check_vma=False,
    )
```

time: 366 us -> 51.7 us (0.14)
  waiting for transfers between devices: 256 us -> 0 us
  Pallas kernels: 0 us -> 45 us
  blocking collectives: 42.4 us -> 0 us
  matrix products: 25.9 us -> 0 us
  local copies, waits for them, and re-layouts: 21 us -> 5.59 us
  between operations: 14.5 us -> 0.65 us
  other arithmetic: 4.98 us -> 0 us
    psum x1 -> x0, waiting for transfers between devices: 105 us -> none  [per_device(): grad_weight, grad_bias = lax.psum((weight_part, bias_part), 'row')]
    unnamed x6 -> x0, waiting for transfers between devices: 91.3 us -> none
    all_gather x1 -> x0, waiting for transfers between devices: 60.4 us -> none  [per_device(): all_projected = lax.all_gather(projected, 'row', axis=1, tiled=True)]
    pallas_call x0 -> x2, Pallas kernels: none -> 45 us  [the longest x1 39.9 us: per_device(): pl.pallas_call(functools.partial(layer_kernel, rz, rp, cn, norm), out_sha...]
    psum x1 -> x0, blocking collectives: 40.4 us -> none  [per_device(): grad_weight, grad_bias = lax.psum((weight_part, bias_part), 'row')]
    dot_general x6 -> x0, matrix products: 25.9 us -> none  [the longest x1 9.68 us: aggregate(): jnp.einsum('fikc,ikrc->fir', picked, tiles.astype(jnp.float32), precision...]
    gather x3 -> x0, local copies, waits for them, and re-layouts: 15.7 us -> none  [the longest x2 14.9 us: aggregate(): picked = jnp.take(shaped, flat_coords, axis=1)]
  transfers between devices with their start and end apart: 4 -> 0, of which waited for: 4 -> 0; matrix products, arithmetic and copies ran while one was open for 2% -> 0% of each run, Pallas kernels for 0% -> 0%
where the time goes in v1:
time: 51.7 us; the launch traced here: 51.3 us
  Pallas kernels  45 us (87%)
  local copies, waits for them, and re-layouts  5.59 us (11%)
  between operations  0.65 us (1%)
    pallas_call x1, Pallas kernels, per_device(): pl.pallas_call(functools.partial(layer_kernel, rz, rp, cn, norm), out_sha...  39.9 us
    unnamed x4, local copies, waits for them, and re-layouts  5.59 us
    pallas_call x1, Pallas kernels, per_device(): pl.pallas_call(build_kernel, out_shape=(dense, dense), in_specs=[anyw, sm...  5.11 us

profile of v1, /device:TPU:0, one launch (start us, length us, event | category | flops | bytes accessed | tf_op | source)
XLA Modules:
  0.0 51.3 jit_solution(16336710599095482110)
XLA Ops:
  0.6 5.1 %build_dense.1 = (bf16[16,256,256]{2,1,0:T(8,128)(2,1)}, bf16[16,256,256]{2,1,0:T(8,128)(2,1)}) custom-call(bf16[2,64,128,128]{3,2,1,0:T(8,128)(2,1)} %tiles.1, s32[2,64]{1,0:T(2,128)} %coords.1, s32[2]{0:T(128)} %counts.1), custom_call_target="tpu_custom_call" | custom-call | tf_op jit(solution)/shard_map/build_dense/pallas_call | solution.py:268
  5.7 39.9 %layer.1 = (bf16[128,256]{1,0:T(8,128)(2,1)}, f32[64,256]{1,0:T(8,128)}, f32[128,128]{1,0:T(8,128)}, f32[1,128]{1,0:T(1,128)}) custom-call(s32[1,256]{1,0:T(1,128)} %bitcast.3, bf16[64,256]{1,0:T(8,128)(2,1)} %feat.1, bf16[128,128]{1,0:T(8,128)(2,1)} %weight.1, bf16[1,128]{1,0:T(2,128)(2,1)} %bitcast.4, bf16[128,256]{1,0:T(8,128)(2,1)} %grad_hidden.1, ...), custom_call_target="tpu_custom_call" | custom-call | tf_op jit(solution)/shard_map/layer/pallas_call | solution.py:289
  45.7 1.5 %copy.16 = bf16[128,256]{1,0:T(8,128)(2,1)} copy(bf16[128,256]{1,0:T(8,128)(2,1)} %get-tuple-element.20) | data formatting | bytes 131072
  47.1 1.5 %copy.17 = f32[64,256]{1,0:T(8,128)} copy(f32[64,256]{1,0:T(8,128)} %get-tuple-element.21) | data formatting | bytes 131072
  48.6 1.5 %copy.18 = f32[128,128]{1,0:T(8,128)} copy(f32[128,128]{1,0:T(8,128)} %get-tuple-element.22) | data formatting | bytes 131072
  50.1 1.2 %copy.19 = f32[128]{0:T(128)} copy(f32[128]{0:T(128)} %bitcast.5) | data formatting | bytes 1024

commit v2 on v1

--- a/solution.py
+++ b/solution.py
@@ -11,6 +11,8 @@
 MESH = pl.DeviceIdType.MESH
 F32 = jnp.float32
 BF16 = jnp.bfloat16
+WIRE = jnp.int16
+TOP = 32000.0
 GROUP = 8
 VMEM_LIMIT = 56 * 1024 * 1024
 
@@ -28,7 +30,18 @@
     return hi, (x - hi.astype(F32)).astype(BF16)
 
 
-def build_kernel(tiles, coords, counts, hi_ref, lo_ref, buf, acc, sems):
+def encode(x, scale):
+    v = jnp.abs(x) * scale
+    u = v * lax.rsqrt(v + 1e-30)
+    return jnp.round(jnp.where(x < 0, -u, u)).astype(jnp.int32).astype(WIRE)
+
+
+def decode(code, unit):
+    u = code.astype(jnp.int32).astype(F32)
+    return u * jnp.abs(u) * unit
+
+
+def build_kernel(tiles, coords, counts, hi_ref, lo_ref, top_ref, buf, acc, sems):
     rows, slots, tile, _ = buf.shape
     groups = slots // GROUP
 
@@ -60,24 +73,27 @@
                 lax.fori_loop(0, live, add, 0)
     pieces = hi_ref.shape[0]
 
-    def convert(p, carry):
+    def convert(p, top):
         for h in range(rows):
-            hi, lo = split(acc[p * rows + h])
+            dense = acc[p * rows + h]
+            hi, lo = split(dense)
+            squares = jnp.sum(dense * dense, axis=0, keepdims=True)
+            top = jnp.maximum(top, jnp.broadcast_to(squares, top.shape))
             hi_ref[p, :, h * tile:(h + 1) * tile] = hi
             lo_ref[p, :, h * tile:(h + 1) * tile] = lo
-        return carry
-
-    lax.fori_loop(0, pieces, convert, 0)
+        return top
+
+    top_ref[...] = lax.fori_loop(0, pieces, convert, jnp.zeros((8, tile), F32))
 
 
 def layer_kernel(
     rz, rp, cn, norm,
-    order, feat, weight, bias, grad_hidden, hi_any, lo_any,
+    order, feat, weight, bias, grad_hidden, top, hi_any, lo_any,
     hid_out, gf_out, gw_out, gb_out,
     ahi, alo, xall, yfull, zpart, zrecv, c1send, c1recv, c2send, c2recv,
-    g1send, g1recv, g2send, g2recv, gall,
+    g1send, g1recv, g2send, g2recv, gall, s1send, s1recv, s2send, s2recv,
     a_sem, x_ss, x_rs, y_ss, y_rs, z_ss, z_rs, c1_ss, c1_rs, c2_ss, c2_rs,
-    g1_ss, g1_rs, g2_ss, g2_rs, g3_ss, g3_rs,
+    g1_ss, g1_rs, g2_ss, g2_rs, g3_ss, g3_rs, s1_ss, s1_rs, s2_ss, s2_rs,
 ):
     row, col = lax.axis_index("row"), lax.axis_index("col")
     zi, pi = row // rp, lax.rem(row, rp)
@@ -192,39 +208,45 @@
     for d in range(1, cn):
         zx[d - 1].wait_recv()
         z = z + zrecv[d]
+    longest = jnp.max(jnp.sum(z * z, axis=1, keepdims=True), axis=0, keepdims=True)
+    bound = jnp.sqrt(longest * jnp.max(top[...], keepdims=True)) + 1e-16
+    s1send[...] = jnp.broadcast_to(bound, s1send.shape)
+    s1 = [go(remote(s1send, s1recv.at[d], s1_ss.at[d], s1_rs.at[d], pmate(d)))
+          for d in range(1, rp)]
+    up = TOP * TOP / bound
     z_hi, z_lo = split(z)
     z_two = jnp.concatenate([z_hi, z_lo], axis=0)
 
     c1 = {}
+    kept = {}
 
     def contribute(d):
         for dp in list(range(1, rp)) + [0]:
             at = lax.rem(zi + d, rz) * rp + lax.rem(pi + dp, rp)
             both = mm(z_two, ahi[at], NN)
-            c1send[d, dp] = both[:fl] + both[fl:] + mm(z_hi, alo[at], NN)
-            if dp:
+            c = both[:fl] + both[fl:] + mm(z_hi, alo[at], NN)
+            if dp == 0:
+                kept[d] = c
+            else:
+                c1send[d, dp] = encode(c, up)
                 c1[d, dp] = go(remote(c1send.at[d, dp], c1recv.at[d, dp], c1_ss.at[d, dp],
                                       c1_rs.at[d, dp], pmate(dp)))
 
     def reduced(d):
-        total = c1send[d, 0]
+        total = kept[d]
         for dp in range(1, rp):
             c1[d, dp].wait_recv()
-            total = total + c1recv[d, dp]
+            total = total + decode(c1recv[d, dp], down[dp])
         return total
 
     c2 = {}
 
     def pass_on(d):
-        c2send[d] = reduced(d)
+        c2send[d] = encode(reduced(d), up2)
         c2[d] = go(remote(c2send.at[d], c2recv.at[d], c2_ss.at[d], c2_rs.at[d], zmate(d)))
 
     contribute(1)
-    for d in range(2, rz):
-        contribute(d)
-        pass_on(d - 1)
-    contribute(0)
-    pass_on(rz - 1)
+    contribute(2)
 
     part = g1send[pi]
     for d in range(1, rp):
@@ -233,7 +255,21 @@
     g2send[...] = part
     g2 = [go(remote(g2send, g2recv.at[d], g2_ss.at[d], g2_rs.at[d], zmate(d)))
           for d in range(1, rz)]
-    total = reduced(0)
+    down = {}
+    for d in range(1, rp):
+        s1[d - 1].wait_recv()
+        down[d] = s1recv[d, :1, :1] * (1.0 / TOP / TOP)
+        bound = bound + s1recv[d, :1, :1]
+    s2send[...] = jnp.broadcast_to(bound, s2send.shape)
+    s2 = [go(remote(s2send, s2recv.at[d], s2_ss.at[d], s2_rs.at[d], zmate(d)))
+          for d in range(1, rz)]
+    up2 = TOP * TOP / bound
+
+    pass_on(1)
+    for d in range(3, rz):
+        contribute(d)
+        pass_on(d - 1)
+    contribute(0)
     for d in range(1, rz):
         g2[d - 1].wait_recv()
         part = part + g2recv[d]
@@ -241,15 +277,24 @@
     g3 = [go(remote(gall.at[pi], gall.at[pi], g3_ss.at[d], g3_rs.at[d], pmate(d)))
           for d in range(1, rp)]
     gb_out[...] = part[fr:fr + 1] * norm
-    for d in range(1, rz):
-        c2[d].wait_recv()
-        total = total + c2recv[d]
-    gf_out[...] = total
+    pass_on(rz - 1)
+    total = reduced(0)
     for c in g3:
         c.wait_recv()
     gw_out[...] = gall[...].reshape(fin, hl) * norm
+    for d in range(1, rz):
+        s2[d - 1].wait_recv()
+        c2[d].wait_recv()
+        total = total + decode(c2recv[d], s2recv[d, :1, :1] * (1.0 / TOP / TOP))
+    gf_out[...] = total
     for c in sent:
         c.wait_send()
+
+
+def hand_over(*refs):
+    half = len(refs) // 2
+    for source, target in zip(refs[:half], refs[half:]):
+        target[...] = source[...]
 
 
 def per_device(r, cn, features, order, weight, bias, tiles, coords, counts, grad_hidden):
@@ -257,7 +302,8 @@
     nodes = order.shape[0]
     fl = features.shape[0]
     fin, hl = weight.shape
-    rz = 4 if r % 4 == 0 else 1
+    rz = 4
+    assert r % rz == 0
     rp = r // rz
     fr = fin // rp
     norm = 1.0 / math.sqrt(nodes * r)
@@ -265,11 +311,11 @@
     smem = pl.BlockSpec(memory_space=pltpu.SMEM)
     anyw = pl.BlockSpec(memory_space=pl.ANY)
     dense = jax.ShapeDtypeStruct((r, nodes, nodes), BF16)
-    hi, lo = pl.pallas_call(
+    hi, lo, top = pl.pallas_call(
         build_kernel,
-        out_shape=(dense, dense),
+        out_shape=(dense, dense, jax.ShapeDtypeStruct((8, tile), F32)),
         in_specs=[anyw, smem, smem],
-        out_specs=(vmem, vmem),
+        out_specs=(vmem, vmem, vmem),
         scratch_shapes=[
             pltpu.VMEM((rows, slots, tile, tile), BF16),
             pltpu.VMEM((r * rows, nodes, tile), F32),
@@ -289,7 +335,7 @@
     hidden, gf, gw, gb = pl.pallas_call(
         functools.partial(layer_kernel, rz, rp, cn, norm),
         out_shape=outs,
-        in_specs=[vmem] * 5 + [anyw] * 2,
+        in_specs=[vmem] * 6 + [anyw] * 2,
         out_specs=(vmem,) * 4,
         scratch_shapes=[
             pltpu.VMEM((r, nodes, nodes), BF16),
@@ -298,15 +344,19 @@
             pltpu.VMEM((fin, nodes), F32),
             pltpu.VMEM((fin, nodes), F32),
             pltpu.VMEM((cn, fl, nodes), F32),
-            pltpu.VMEM((rz, rp, fl, nodes), F32),
-            pltpu.VMEM((rz, rp, fl, nodes), F32),
-            pltpu.VMEM((rz, fl, nodes), F32),
-            pltpu.VMEM((rz, fl, nodes), F32),
+            pltpu.VMEM((rz, rp, fl, nodes), WIRE),
+            pltpu.VMEM((rz, rp, fl, nodes), WIRE),
+            pltpu.VMEM((rz, fl, nodes), WIRE),
+            pltpu.VMEM((rz, fl, nodes), WIRE),
             pltpu.VMEM((rp, fr + 8, hl), F32),
             pltpu.VMEM((rp, fr + 8, hl), F32),
             pltpu.VMEM((fr + 8, hl), F32),
             pltpu.VMEM((rz, fr + 8, hl), F32),
             pltpu.VMEM((rp, fr, hl), F32),
+            pltpu.VMEM((8, 128), F32),
+            pltpu.VMEM((rp, 8, 128), F32),
+            pltpu.VMEM((8, 128), F32),
+            pltpu.VMEM((rz, 8, 128), F32),
             dma((2,)),
             dma((rz, rp)), dma((rz, rp)),
             dma((cn,)), dma((cn,)),
@@ -316,12 +366,21 @@
             dma((rp,)), dma((rp,)),
             dma((rz,)), dma((rz,)),
             dma((rp,)), dma((rp,)),
+            dma((rp,)), dma((rp,)),
+            dma((rz,)), dma((rz,)),
         ],
         compiler_params=pltpu.CompilerParams(
             collective_id=0, has_side_effects=True, vmem_limit_bytes=VMEM_LIMIT
         ),
         name="layer",
-    )(order.reshape(1, nodes), features, weight, bias.reshape(1, hl), grad_hidden, hi, lo)
+    )(order.reshape(1, nodes), features, weight, bias.reshape(1, hl), grad_hidden, top, hi, lo)
+    hidden, gf, gw, gb = pl.pallas_call(
+        hand_over,
+        out_shape=outs,
+        in_specs=[vmem] * 4,
+        out_specs=(vmem,) * 4,
+        name="hand_over",
+    )(hidden, gf, gw, gb)
     return hidden, gf, gw, gb.reshape(hl)
 
 

time: 51.7 us -> 39.5 us (0.76)
  Pallas kernels: 45 us -> 38.3 us
  local copies, waits for them, and re-layouts: 5.59 us -> 0 us
    pallas_call x1, Pallas kernels: 39.9 us -> 31 us  [per_device(): pl.pallas_call(functools.partial(layer_kernel, rz, rp, cn, norm), out_sha...]
    unnamed x4 -> x0, local copies, waits for them, and re-layouts: 5.59 us -> none
    pallas_call x1 -> x2, Pallas kernels: 5.11 us -> 7.33 us  [the longest x1 5.74 us: per_device(): pl.pallas_call(build_kernel, out_shape=(dense, dense, jax.ShapeDtypeStruc...]
where the time goes in v2:
time: 39.5 us; the launch traced here: 39 us
  Pallas kernels  38.3 us (97%)
  between operations  0.65 us (2%)
    pallas_call x1, Pallas kernels, per_device(): pl.pallas_call(functools.partial(layer_kernel, rz, rp, cn, norm), out_sha...  31 us
    pallas_call x1, Pallas kernels, per_device(): pl.pallas_call(build_kernel, out_shape=(dense, dense, jax.ShapeDtypeStruc...  5.74 us
    pallas_call x1, Pallas kernels, per_device(): pl.pallas_call(hand_over, out_shape=outs, in_specs=[vmem] * 4, out_specs=...  1.59 us

profile of v2, /device:TPU:0, one launch (start us, length us, event | category | flops | bytes accessed | tf_op | source)
XLA Modules:
  0.0 39.0 jit_solution(3184432883971046977)
XLA Ops:
  0.6 5.7 %build_dense.1 = (bf16[16,256,256]{2,1,0:T(8,128)(2,1)}, bf16[16,256,256]{2,1,0:T(8,128)(2,1)}, f32[8,128]{1,0:T(8,128)}) custom-call(bf16[2,64,128,128]{3,2,1,0:T(8,128)(2,1)} %tiles.1, s32[2,64]{1,0:T(2,128)} %coords.1, s32[2]{0:T(128)} %counts.1), custom_call_target="tpu_custom_call" | custom-call | tf_op jit(solution)/shard_map/build_dense/pallas_call | solution.py:314
  6.4 31.0 %layer.1 = (bf16[128,256]{1,0:T(8,128)(2,1)}, f32[64,256]{1,0:T(8,128)}, f32[128,128]{1,0:T(8,128)}, f32[1,128]{1,0:T(1,128)}) custom-call(s32[1,256]{1,0:T(1,128)} %bitcast.3, bf16[64,256]{1,0:T(8,128)(2,1)} %feat.1, bf16[128,128]{1,0:T(8,128)(2,1)} %weight.1, bf16[1,128]{1,0:T(2,128)(2,1)} %bitcast.4, bf16[128,256]{1,0:T(8,128)(2,1)} %grad_hidden.1, ...), custom_call_target="tpu_custom_call" | custom-call | tf_op jit(solution)/shard_map/layer/pallas_call | solution.py:335
  37.4 1.6 %hand_over.1 = (bf16[128,256]{1,0:T(8,128)(2,1)}, f32[64,256]{1,0:T(8,128)}, f32[128,128]{1,0:T(8,128)}, f32[1,128]{1,0:T(1,128)}) custom-call(bf16[128,256]{1,0:T(8,128)(2,1)} %get-tuple-element.18.refs_0_, f32[64,256]{1,0:T(8,128)} %get-tuple-element.19.refs_1_, f32[128,128]{1,0:T(8,128)} %get-tuple-element.20.refs_2_, f32[1,128]{1,0:T(1,128)} %get-tuple-element.21.refs_3_), custom_call_target="tpu_custom_call" | custom-call | tf_op jit(solution)/shard_map/hand_over/pallas_call | solution.py:377

commit v3 on v2

--- a/solution.py
+++ b/solution.py
@@ -13,7 +13,6 @@
 BF16 = jnp.bfloat16
 WIRE = jnp.int16
 TOP = 32000.0
-GROUP = 8
 VMEM_LIMIT = 56 * 1024 * 1024
 
 NN = (((1,), (0,)), ((), ()))
@@ -41,56 +40,35 @@
     return u * jnp.abs(u) * unit
 
 
-def build_kernel(tiles, coords, counts, hi_ref, lo_ref, top_ref, buf, acc, sems):
-    rows, slots, tile, _ = buf.shape
-    groups = slots // GROUP
-
-    def copy(i, g):
-        part = pl.ds(g * GROUP, GROUP)
-        return pltpu.make_async_copy(tiles.at[i, part], buf.at[i, part], sems.at[i, g])
-
-    for g in range(groups):
-        for i in range(rows):
-            @pl.when(counts[i] > g * GROUP)
-            def _():
-                copy(i, g).start()
-    acc[...] = jnp.zeros_like(acc)
-    for g in range(groups):
-        for i in range(rows):
-            live = jnp.clip(counts[i] - g * GROUP, 0, GROUP)
-
-            @pl.when(live > 0)
-            def _():
-                copy(i, g).wait()
-
-                def add(k, carry):
-                    at = g * GROUP + k
-                    j = coords[i, at]
-                    mine = pl.ds(i * tile, tile)
-                    acc[j, mine, :] = acc[j, mine, :] + buf[i, at].astype(F32)
-                    return carry
-
-                lax.fori_loop(0, live, add, 0)
-    pieces = hi_ref.shape[0]
-
-    def convert(p, top):
-        for h in range(rows):
-            dense = acc[p * rows + h]
-            hi, lo = split(dense)
-            squares = jnp.sum(dense * dense, axis=0, keepdims=True)
-            top = jnp.maximum(top, jnp.broadcast_to(squares, top.shape))
-            hi_ref[p, :, h * tile:(h + 1) * tile] = hi
-            lo_ref[p, :, h * tile:(h + 1) * tile] = lo
-        return top
-
-    top_ref[...] = lax.fori_loop(0, pieces, convert, jnp.zeros((8, tile), F32))
+def slot_table(coords, count):
+    slots = coords.shape[1]
+    sub = lax.broadcasted_iota(jnp.int32, (slots, slots), 0)
+    lane = lax.broadcasted_iota(jnp.int32, (slots, slots), 1)
+    dead = 1 << 12
+    key = jnp.where(lane < count, jnp.broadcast_to(coords, (slots, slots)), dead)
+    flip = jnp.sum(jnp.where(sub == lane, key, 0), axis=1, keepdims=True)
+    same = (key == flip) & (lane < sub)
+    ahead = jnp.sum(jnp.where((key < flip) | same, 1, 0), axis=1, keepdims=True)
+    keep = jnp.minimum(jnp.sum(jnp.where(same, 1, 0), axis=1, keepdims=True), 1)
+    place = lax.broadcasted_iota(jnp.int32, (slots, 128), 1)
+    slot = lax.broadcasted_iota(jnp.int32, (slots, 128), 0)
+    match = ahead == place
+
+    def down(x):
+        return jnp.sum(x, axis=0, keepdims=True)
+
+    order = down(jnp.where(match, slot, 0))
+    goes_on = down(jnp.where(match, keep, 0))
+    last = jnp.maximum(down(jnp.where(flip <= place, 1, 0)) - 1, 0)
+    named = jnp.minimum(down(jnp.where(flip == place, 1, 0)), 1)
+    return [order, goes_on, last, named]
 
 
 def layer_kernel(
     rz, rp, cn, norm,
-    order, feat, weight, bias, grad_hidden, top, hi_any, lo_any,
+    order, feat, weight, bias, grad_hidden, coords, counts, tiles,
     hid_out, gf_out, gw_out, gb_out,
-    ahi, alo, xall, yfull, zpart, zrecv, c1send, c1recv, c2send, c2recv,
+    buf, run, table, places, ahi, alo, xall, yfull, zpart, zrecv, c1send, c1recv, c2send, c2recv,
     g1send, g1recv, g2send, g2recv, gall, s1send, s1recv, s2send, s2recv,
     a_sem, x_ss, x_rs, y_ss, y_rs, z_ss, z_rs, c1_ss, c1_rs, c2_ss, c2_rs,
     g1_ss, g1_rs, g2_ss, g2_rs, g3_ss, g3_rs, s1_ss, s1_rs, s2_ss, s2_rs,
@@ -121,13 +99,20 @@
             device_id=to, device_id_type=MESH,
         )
 
-    load_hi = pltpu.make_async_copy(hi_any, ahi, a_sem.at[0])
-    load_lo = pltpu.make_async_copy(lo_any, alo, a_sem.at[1])
-    load_hi.start()
-    load_lo.start()
+    rows, slots, tile, _ = buf.shape
+    loads = [pltpu.make_async_copy(tiles.at[i], buf.at[i], a_sem.at[i]) for i in range(rows)]
+    for c in loads:
+        c.start()
     barrier = pltpu.get_barrier_semaphore()
     for mate in mates:
         pl.semaphore_signal(barrier, inc=1, device_id=mate, device_id_type=MESH)
+
+    lines = []
+    for i in range(rows):
+        lines += slot_table(coords[i:i + 1, :], counts[i])
+    table[...] = jnp.concatenate(lines, axis=0)
+    to_places = pltpu.make_async_copy(table, places, a_sem.at[rows])
+    to_places.start()
 
     local = order[...] - row * nodes
     pick = (lax.broadcasted_iota(jnp.int32, (nodes, nodes), 0) == local).astype(F32).astype(BF16)
@@ -151,8 +136,43 @@
                                    x_rs.at[dz, dp], pmate(dp)))
 
     relay(0)
-    load_hi.wait()
-    load_lo.wait()
+    to_places.wait()
+    for c in loads:
+        c.wait()
+
+    def add(s, sums):
+        new = []
+        for i in range(rows):
+            keep = places[4 * i + 1, s].astype(F32)
+            total = sums[i] * keep + buf[i, jnp.clip(places[4 * i, s], 0, slots - 1)].astype(F32)
+            run[i, s] = total
+            new.append(total)
+        return tuple(new)
+
+    sums = tuple(jnp.zeros((tile, tile), F32) for _ in range(rows))
+    near = [1, 3, 2]
+    step = slots // 4
+    for n in range(4):
+        sums = lax.fori_loop(n * step, (n + 1) * step, add, sums)
+        if n < 3:
+            xz[near[n]].wait_recv()
+            relay(near[n])
+
+    def place(p, top):
+        for h in range(rows):
+            squares = jnp.zeros((1, tile), F32)
+            for i in range(rows):
+                j = p * rows + h
+                named = places[4 * i + 3, j].astype(F32)
+                dense = run[i, jnp.clip(places[4 * i + 2, j], 0, slots - 1)] * named
+                hi, lo = split(dense)
+                ahi[p, i * tile:(i + 1) * tile, h * tile:(h + 1) * tile] = hi
+                alo[p, i * tile:(i + 1) * tile, h * tile:(h + 1) * tile] = lo
+                squares = squares + jnp.sum(dense * dense, axis=0, keepdims=True)
+            top = jnp.maximum(top, squares)
+        return top
+
+    top = lax.fori_loop(0, rz * rp, place, jnp.zeros((1, tile), F32))
 
     def piece(dz, dp):
         return lax.rem(zi + rz - dz, rz) * rp + lax.rem(pi + rp - dp, rp)
@@ -163,11 +183,9 @@
         return mm(x, ahi[at], NT) + mm(x, alo[at], NT)
 
     y = term(0, 0)
-    for dz in range(1, rz):
-        xz[dz].wait_recv()
-        relay(dz)
+    for dz in near:
         y = y + term(dz, 0)
-    for dz in range(rz):
+    for dz in [0] + near:
         for dp in range(1, rp):
             xp[dz, dp].wait_recv()
             y = y + term(dz, dp)
@@ -209,7 +227,7 @@
         zx[d - 1].wait_recv()
         z = z + zrecv[d]
     longest = jnp.max(jnp.sum(z * z, axis=1, keepdims=True), axis=0, keepdims=True)
-    bound = jnp.sqrt(longest * jnp.max(top[...], keepdims=True)) + 1e-16
+    bound = jnp.sqrt(longest * jnp.max(top, keepdims=True)) + 1e-16
     s1send[...] = jnp.broadcast_to(bound, s1send.shape)
     s1 = [go(remote(s1send, s1recv.at[d], s1_ss.at[d], s1_rs.at[d], pmate(d)))
           for d in range(1, rp)]
@@ -303,28 +321,13 @@
     fl = features.shape[0]
     fin, hl = weight.shape
     rz = 4
-    assert r % rz == 0
+    assert r % rz == 0 and slots % 4 == 0 and r * rows <= 128
     rp = r // rz
     fr = fin // rp
     norm = 1.0 / math.sqrt(nodes * r)
     vmem = pl.BlockSpec(memory_space=pltpu.VMEM)
     smem = pl.BlockSpec(memory_space=pltpu.SMEM)
     anyw = pl.BlockSpec(memory_space=pl.ANY)
-    dense = jax.ShapeDtypeStruct((r, nodes, nodes), BF16)
-    hi, lo, top = pl.pallas_call(
-        build_kernel,
-        out_shape=(dense, dense, jax.ShapeDtypeStruct((8, tile), F32)),
-        in_specs=[anyw, smem, smem],
-        out_specs=(vmem, vmem, vmem),
-        scratch_shapes=[
-            pltpu.VMEM((rows, slots, tile, tile), BF16),
-            pltpu.VMEM((r * rows, nodes, tile), F32),
-            pltpu.SemaphoreType.DMA((rows, slots // GROUP)),
-        ],
-        compiler_params=pltpu.CompilerParams(vmem_limit_bytes=VMEM_LIMIT),
-        name="build_dense",
-    )(tiles, coords, counts)
-
     dma = pltpu.SemaphoreType.DMA
     outs = (
         jax.ShapeDtypeStruct((hl, nodes), BF16),
@@ -335,9 +338,13 @@
     hidden, gf, gw, gb = pl.pallas_call(
         functools.partial(layer_kernel, rz, rp, cn, norm),
         out_shape=outs,
-        in_specs=[vmem] * 6 + [anyw] * 2,
+        in_specs=[vmem] * 6 + [smem, anyw],
         out_specs=(vmem,) * 4,
         scratch_shapes=[
+            pltpu.VMEM((rows, slots, tile, tile), BF16),
+            pltpu.VMEM((rows, slots, tile, tile), F32),
+            pltpu.VMEM((4 * rows, 128), jnp.int32),
+            pltpu.SMEM((4 * rows, 128), jnp.int32),
             pltpu.VMEM((r, nodes, nodes), BF16),
             pltpu.VMEM((r, nodes, nodes), BF16),
             pltpu.VMEM((rz, rp, fl, nodes), BF16),
@@ -357,7 +364,7 @@
             pltpu.VMEM((rp, 8, 128), F32),
             pltpu.VMEM((8, 128), F32),
             pltpu.VMEM((rz, 8, 128), F32),
-            dma((2,)),
+            dma((rows + 1,)),
             dma((rz, rp)), dma((rz, rp)),
             dma((cn,)), dma((cn,)),
             dma((cn,)), dma((cn,)),
@@ -373,7 +380,7 @@
             collective_id=0, has_side_effects=True, vmem_limit_bytes=VMEM_LIMIT
         ),
         name="layer",
-    )(order.reshape(1, nodes), features, weight, bias.reshape(1, hl), grad_hidden, top, hi, lo)
+    )(order.reshape(1, nodes), features, weight, bias.reshape(1, hl), grad_hidden, coords, counts, tiles)
     hidden, gf, gw, gb = pl.pallas_call(
         hand_over,
         out_shape=outs,

time: 39.5 us -> 34 us (0.86)
  Pallas kernels: 38.3 us -> 33.2 us
    pallas_call x1 -> x0, Pallas kernels: 5.74 us -> none  [per_device(): pl.pallas_call(build_kernel, out_shape=(dense, dense, jax.ShapeDtypeStruc...]
    pallas_call x1, Pallas kernels: 31 us -> 31.6 us  [per_device(): pl.pallas_call(functools.partial(layer_kernel, rz, rp, cn, norm), out_sha...]
where the time goes in v3:
time: 34 us; the launch traced here: 33.8 us
  Pallas kernels  33.2 us (98%)
  between operations  0.64 us (2%)
    pallas_call x1, Pallas kernels, per_device(): pl.pallas_call(functools.partial(layer_kernel, rz, rp, cn, norm), out_sha...  31.6 us
    pallas_call x1, Pallas kernels, per_device(): pl.pallas_call(hand_over, out_shape=outs, in_specs=[vmem] * 4, out_specs=...  1.59 us

profile of v3, /device:TPU:0, one launch (start us, length us, event | category | flops | bytes accessed | tf_op | source)
XLA Modules:
  0.0 33.8 jit_solution(6233784610588230005)
XLA Ops:
  0.6 31.6 %layer.1 = (bf16[128,256]{1,0:T(8,128)(2,1)}, f32[64,256]{1,0:T(8,128)}, f32[128,128]{1,0:T(8,128)}, f32[1,128]{1,0:T(1,128)}) custom-call(s32[1,256]{1,0:T(1,128)} %bitcast.3, bf16[64,256]{1,0:T(8,128)(2,1)} %feat.1, bf16[128,128]{1,0:T(8,128)(2,1)} %weight.1, bf16[1,128]{1,0:T(2,128)(2,1)} %bitcast.4, bf16[128,256]{1,0:T(8,128)(2,1)} %grad_hidden.1, ...), custom_call_target="tpu_custom_call" | custom-call | tf_op jit(solution)/shard_map/layer/pallas_call | solution.py:338
  32.2 1.6 %hand_over.1 = (bf16[128,256]{1,0:T(8,128)(2,1)}, f32[64,256]{1,0:T(8,128)}, f32[128,128]{1,0:T(8,128)}, f32[1,128]{1,0:T(1,128)}) custom-call(bf16[128,256]{1,0:T(8,128)(2,1)} %get-tuple-element.12.refs_0_, f32[64,256]{1,0:T(8,128)} %get-tuple-element.13.refs_1_, f32[128,128]{1,0:T(8,128)} %get-tuple-element.14.refs_2_, f32[1,128]{1,0:T(1,128)} %get-tuple-element.15.refs_3_), custom_call_target="tpu_custom_call" | custom-call | tf_op jit(solution)/shard_map/hand_over/pallas_call | solution.py:384

commit v4 on v3

--- a/solution.py
+++ b/solution.py
@@ -68,9 +68,9 @@
     rz, rp, cn, norm,
     order, feat, weight, bias, grad_hidden, coords, counts, tiles,
     hid_out, gf_out, gw_out, gb_out,
-    buf, run, table, places, ahi, alo, xall, yfull, zpart, zrecv, c1send, c1recv, c2send, c2recv,
+    buf, run, table, places, ahi, alo, xall, yfull, wall, hall, c1send, c1recv, c2send, c2recv,
     g1send, g1recv, g2send, g2recv, gall, s1send, s1recv, s2send, s2recv,
-    a_sem, x_ss, x_rs, y_ss, y_rs, z_ss, z_rs, c1_ss, c1_rs, c2_ss, c2_rs,
+    a_sem, x_ss, x_rs, y_ss, y_rs, w_ss, w_rs, h_ss, h_rs, c1_ss, c1_rs, c2_ss, c2_rs,
     g1_ss, g1_rs, g2_ss, g2_rs, g3_ss, g3_rs, s1_ss, s1_rs, s2_ss, s2_rs,
 ):
     row, col = lax.axis_index("row"), lax.axis_index("col")
@@ -117,6 +117,9 @@
     local = order[...] - row * nodes
     pick = (lax.broadcasted_iota(jnp.int32, (nodes, nodes), 0) == local).astype(F32).astype(BF16)
     xall[0, 0] = mm(feat[...], pick, NN).astype(BF16)
+    first = lax.broadcasted_iota(jnp.int32, (16, hl), 0) == 0
+    wall[0, :fin, :] = weight[...]
+    wall[0, fin:, :] = jnp.where(first, bias[...].astype(F32), 0.0).astype(BF16)
     pl.semaphore_wait(barrier, len(mates))
 
     sent = []
@@ -136,6 +139,10 @@
                                    x_rs.at[dz, dp], pmate(dp)))
 
     relay(0)
+    wx = [go(remote(wall.at[0], wall.at[d], w_ss.at[d], w_rs.at[d], cmate(d)))
+          for d in range(1, cn)]
+    hx = [go(remote(grad_hidden, hall.at[d], h_ss.at[d], h_rs.at[d], cmate(d)))
+          for d in range(1, cn)]
     to_places.wait()
     for c in loads:
         c.wait()
@@ -153,7 +160,7 @@
     near = [1, 3, 2]
     step = slots // 4
     for n in range(4):
-        sums = lax.fori_loop(n * step, (n + 1) * step, add, sums)
+        sums = lax.fori_loop(n * step, (n + 1) * step, add, sums, unroll=4)
         if n < 3:
             xz[near[n]].wait_recv()
             relay(near[n])
@@ -172,23 +179,20 @@
             top = jnp.maximum(top, squares)
         return top
 
-    top = lax.fori_loop(0, rz * rp, place, jnp.zeros((1, tile), F32))
-
     def piece(dz, dp):
         return lax.rem(zi + rz - dz, rz) * rp + lax.rem(pi + rp - dp, rp)
 
-    def term(dz, dp):
+    order_in = [(0, 0)] + [(dz, 0) for dz in near]
+    order_in += [(dz, dp) for dz in [0] + near for dp in range(1, rp)]
+    top = jnp.zeros((1, tile), F32)
+    y = jnp.zeros((fl, nodes), F32)
+    for dz, dp in order_in:
         at = piece(dz, dp)
+        top = place(at, top)
+        if dp:
+            xp[dz, dp].wait_recv()
         x = xall[dz, dp]
-        return mm(x, ahi[at], NT) + mm(x, alo[at], NT)
-
-    y = term(0, 0)
-    for dz in near:
-        y = y + term(dz, 0)
-    for dz in [0] + near:
-        for dp in range(1, rp):
-            xp[dz, dp].wait_recv()
-            y = y + term(dz, dp)
+        y = y + mm(x, ahi[at], NT) + mm(x, alo[at], NT)
 
     mine = pl.ds(pl.multiple_of(col * fl, fl), fl)
     yfull[mine, :] = y
@@ -196,36 +200,24 @@
           for d in range(1, cn)]
     for c in yx:
         c.wait_recv()
+    for c in wx + hx:
+        c.wait_recv()
     y_hi, y_lo = split(yfull[...])
-
-    w = weight[...]
-    first = lax.broadcasted_iota(jnp.int32, (16, hl), 0) == 0
-    bias_rows = jnp.where(first, bias[...].astype(F32), 0.0).astype(BF16)
-    pre = mm(w, y_hi, TN) + mm(w, y_lo, TN) + mm(bias_rows, jnp.ones((16, nodes), BF16), TN)
-    gate = jax.nn.sigmoid(pre)
-    hid_out[...] = (pre * gate).astype(BF16)
-    grad_pre = grad_hidden[...].astype(F32) * gate * (1.0 + pre * (1.0 - gate))
-    gp_hi, gp_lo = split(grad_pre)
-
-    zpart[...] = mm(w, gp_hi, NN) + mm(w, gp_lo, NN)
-    zx = []
-    for d in range(1, cn):
-        theirs = pl.ds(pl.multiple_of(lax.rem(col + d, cn) * fl, fl), fl)
-        zx.append(go(remote(zpart.at[theirs], zrecv.at[d], z_ss.at[d], z_rs.at[d], cmate(d))))
-
-    gw = mm(y_hi, gp_hi, NT) + mm(y_lo, gp_hi, NT) + mm(y_hi, gp_lo, NT)
     ones = jnp.ones((16, nodes), BF16)
-    gb = (mm(ones, gp_hi, NT) + mm(ones, gp_lo, NT))[:8]
-    for q in range(rp):
-        g1send[q, :fr] = gw[q * fr:(q + 1) * fr]
-        g1send[q, fr:] = gb
-    g1 = [go(remote(g1send.at[lax.rem(pi + d, rp)], g1recv.at[d], g1_ss.at[d], g1_rs.at[d],
-                    pmate(d))) for d in range(1, rp)]
-
-    z = zpart[mine, :]
-    for d in range(1, cn):
-        zx[d - 1].wait_recv()
-        z = z + zrecv[d]
+    y_ext = jnp.concatenate([y_hi, ones], axis=0)
+
+    z = jnp.zeros((fl, nodes), F32)
+    for d in range(cn):
+        pre = mm(wall[d], y_ext, TN) + mm(wall[d, :fin, :], y_lo, TN)
+        gate = jax.nn.sigmoid(pre)
+        cotangent = grad_hidden[...] if d == 0 else hall[d]
+        grad_pre = cotangent.astype(F32) * gate * (1.0 + pre * (1.0 - gate))
+        part_hi, part_lo = split(grad_pre)
+        z = z + mm(wall[d, mine, :], part_hi, NN) + mm(wall[d, mine, :], part_lo, NN)
+        if d == 0:
+            hid_out[...] = (pre * gate).astype(BF16)
+            gp_hi, gp_lo = part_hi, part_lo
+
     longest = jnp.max(jnp.sum(z * z, axis=1, keepdims=True), axis=0, keepdims=True)
     bound = jnp.sqrt(longest * jnp.max(top, keepdims=True)) + 1e-16
     s1send[...] = jnp.broadcast_to(bound, s1send.shape)
@@ -264,15 +256,17 @@
         c2[d] = go(remote(c2send.at[d], c2recv.at[d], c2_ss.at[d], c2_rs.at[d], zmate(d)))
 
     contribute(1)
+
+    gw = mm(y_ext, gp_hi, NT) + mm(y_ext, gp_lo, NT)
+    gb = gw[fin:fin + 8]
+    gw = gw[:fin] + mm(y_lo, gp_hi, NT)
+    for q in range(rp):
+        g1send[q, :fr] = gw[q * fr:(q + 1) * fr]
+        g1send[q, fr:] = gb
+    g1 = [go(remote(g1send.at[lax.rem(pi + d, rp)], g1recv.at[d], g1_ss.at[d], g1_rs.at[d],
+                    pmate(d))) for d in range(1, rp)]
     contribute(2)
 
-    part = g1send[pi]
-    for d in range(1, rp):
-        g1[d - 1].wait_recv()
-        part = part + g1recv[d]
-    g2send[...] = part
-    g2 = [go(remote(g2send, g2recv.at[d], g2_ss.at[d], g2_rs.at[d], zmate(d)))
-          for d in range(1, rz)]
     down = {}
     for d in range(1, rp):
         s1[d - 1].wait_recv()
@@ -287,6 +281,13 @@
     for d in range(3, rz):
         contribute(d)
         pass_on(d - 1)
+    part = g1send[pi]
+    for d in range(1, rp):
+        g1[d - 1].wait_recv()
+        part = part + g1recv[d]
+    g2send[...] = part
+    g2 = [go(remote(g2send, g2recv.at[d], g2_ss.at[d], g2_rs.at[d], zmate(d)))
+          for d in range(1, rz)]
     contribute(0)
     for d in range(1, rz):
         g2[d - 1].wait_recv()
@@ -310,9 +311,13 @@
 
 
 def hand_over(*refs):
+    sems = refs[-1]
     half = len(refs) // 2
-    for source, target in zip(refs[:half], refs[half:]):
-        target[...] = source[...]
+    copies = [pltpu.make_async_copy(refs[n], refs[half + n], sems.at[n]) for n in range(half)]
+    for c in copies:
+        c.start()
+    for c in copies:
+        c.wait()
 
 
 def per_device(r, cn, features, order, weight, bias, tiles, coords, counts, grad_hidden):
@@ -349,8 +354,8 @@
             pltpu.VMEM((r, nodes, nodes), BF16),
             pltpu.VMEM((rz, rp, fl, nodes), BF16),
             pltpu.VMEM((fin, nodes), F32),
-            pltpu.VMEM((fin, nodes), F32),
-            pltpu.VMEM((cn, fl, nodes), F32),
+            pltpu.VMEM((cn, fin + 16, hl), BF16),
+            pltpu.VMEM((cn, hl, nodes), BF16),
             pltpu.VMEM((rz, rp, fl, nodes), WIRE),
             pltpu.VMEM((rz, rp, fl, nodes), WIRE),
             pltpu.VMEM((rz, fl, nodes), WIRE),
@@ -366,6 +371,7 @@
             pltpu.VMEM((rz, 8, 128), F32),
             dma((rows + 1,)),
             dma((rz, rp)), dma((rz, rp)),
+            dma((cn,)), dma((cn,)),
             dma((cn,)), dma((cn,)),
             dma((cn,)), dma((cn,)),
             dma((rz, rp)), dma((rz, rp)),
@@ -384,8 +390,9 @@
     hidden, gf, gw, gb = pl.pallas_call(
         hand_over,
         out_shape=outs,
-        in_specs=[vmem] * 4,
-        out_specs=(vmem,) * 4,
+        in_specs=[anyw] * 4,
+        out_specs=(anyw,) * 4,
+        scratch_shapes=[dma((4,))],
         name="hand_over",
     )(hidden, gf, gw, gb)
     return hidden, gf, gw, gb.reshape(hl)

time: 34 us -> 41.7 us (1.23)
  Pallas kernels: 33.2 us -> 40.9 us
    pallas_call x1, Pallas kernels: 1.59 us -> 7.11 us  [per_device(): pl.pallas_call(hand_over, out_shape=outs, in_specs=[anyw] * 4, out_specs=...]
    pallas_call x1, Pallas kernels: 31.6 us -> 33.8 us  [per_device(): pl.pallas_call(functools.partial(layer_kernel, rz, rp, cn, norm), out_sha...]
where the time goes in v4:
time: 41.7 us; the launch traced here: 41.5 us
  Pallas kernels  40.9 us (98%)
  between operations  0.64 us (2%)
    pallas_call x1, Pallas kernels, per_device(): pl.pallas_call(functools.partial(layer_kernel, rz, rp, cn, norm), out_sha...  33.8 us
    pallas_call x1, Pallas kernels, per_device(): pl.pallas_call(hand_over, out_shape=outs, in_specs=[anyw] * 4, out_specs=...  7.11 us

profile of v4, /device:TPU:0, one launch (start us, length us, event | category | flops | bytes accessed | tf_op | source)
XLA Modules:
  0.0 41.5 jit_solution(12084282863086421595)
XLA Ops:
  0.6 33.8 %layer.1 = (bf16[128,256]{1,0:T(8,128)(2,1)}, f32[64,256]{1,0:T(8,128)}, f32[128,128]{1,0:T(8,128)}, f32[1,128]{1,0:T(1,128)}) custom-call(s32[1,256]{1,0:T(1,128)} %bitcast.3, bf16[64,256]{1,0:T(8,128)(2,1)} %feat.1, bf16[128,128]{1,0:T(8,128)(2,1)} %weight.1, bf16[1,128]{1,0:T(2,128)(2,1)} %bitcast.4, bf16[128,256]{1,0:T(8,128)(2,1)} %grad_hidden.1, ...), custom_call_target="tpu_custom_call" | custom-call | tf_op jit(solution)/shard_map/layer/pallas_call | solution.py:343
  34.4 7.1 %hand_over.1 = (bf16[128,256]{1,0:T(8,128)(2,1)}, f32[64,256]{1,0:T(8,128)}, f32[128,128]{1,0:T(8,128)}, f32[1,128]{1,0:T(1,128)}) custom-call(bf16[128,256]{1,0:T(8,128)(2,1)} %get-tuple-element.12.refs_0_, f32[64,256]{1,0:T(8,128)} %get-tuple-element.13.refs_1_, f32[128,128]{1,0:T(8,128)} %get-tuple-element.14.refs_2_, f32[1,128]{1,0:T(1,128)} %get-tuple-element.15.refs_3_), custom_call_target="tpu_custom_call" | custom-call | tf_op jit(solution)/shard_map/hand_over/pallas_call | solution.py:390

commit v5 on v4

--- a/solution.py
+++ b/solution.py
@@ -68,7 +68,7 @@
     rz, rp, cn, norm,
     order, feat, weight, bias, grad_hidden, coords, counts, tiles,
     hid_out, gf_out, gw_out, gb_out,
-    buf, run, table, places, ahi, alo, xall, yfull, wall, hall, c1send, c1recv, c2send, c2recv,
+    buf, run, table, places, ahi, alo, xall, yfull, wall, hall, gp, kept, c1send, c1recv, c2send, c2recv,
     g1send, g1recv, g2send, g2recv, gall, s1send, s1recv, s2send, s2recv,
     a_sem, x_ss, x_rs, y_ss, y_rs, w_ss, w_rs, h_ss, h_rs, c1_ss, c1_rs, c2_ss, c2_rs,
     g1_ss, g1_rs, g2_ss, g2_rs, g3_ss, g3_rs, s1_ss, s1_rs, s2_ss, s2_rs,
@@ -119,6 +119,7 @@
     xall[0, 0] = mm(feat[...], pick, NN).astype(BF16)
     first = lax.broadcasted_iota(jnp.int32, (16, hl), 0) == 0
     wall[0, :fin, :] = weight[...]
+    hall[0] = grad_hidden[...]
     wall[0, fin:, :] = jnp.where(first, bias[...].astype(F32), 0.0).astype(BF16)
     pl.semaphore_wait(barrier, len(mates))
 
@@ -129,19 +130,28 @@
         sent.append(c)
         return c
 
-    xz = {d: go(remote(xall.at[0, 0], xall.at[d, 0], x_ss.at[d, 0], x_rs.at[d, 0], zmate(d)))
-          for d in range(1, rz)}
-    xp = {}
+    def each(low, high, body, unroll=1):
+        def run_body(n, carry):
+            body(n)
+            return carry
+
+        lax.fori_loop(low, high, run_body, 0, unroll=unroll)
+
+    def xz(d):
+        return remote(xall.at[0, 0], xall.at[d, 0], x_ss.at[d, 0], x_rs.at[d, 0], zmate(d))
+
+    def xp(dz, dp):
+        return remote(xall.at[dz, 0], xall.at[dz, dp], x_ss.at[dz, dp], x_rs.at[dz, dp],
+                      pmate(dp))
 
     def relay(dz):
-        for dp in range(1, rp):
-            xp[dz, dp] = go(remote(xall.at[dz, 0], xall.at[dz, dp], x_ss.at[dz, dp],
-                                   x_rs.at[dz, dp], pmate(dp)))
-
+        each(1, rp, lambda dp: xp(dz, dp).start())
+
+    each(1, rz, lambda d: xz(d).start())
     relay(0)
     wx = [go(remote(wall.at[0], wall.at[d], w_ss.at[d], w_rs.at[d], cmate(d)))
           for d in range(1, cn)]
-    hx = [go(remote(grad_hidden, hall.at[d], h_ss.at[d], h_rs.at[d], cmate(d)))
+    hx = [go(remote(hall.at[0], hall.at[d], h_ss.at[d], h_rs.at[d], cmate(d)))
           for d in range(1, cn)]
     to_places.wait()
     for c in loads:
@@ -157,13 +167,16 @@
         return tuple(new)
 
     sums = tuple(jnp.zeros((tile, tile), F32) for _ in range(rows))
-    near = [1, 3, 2]
-    step = slots // 4
-    for n in range(4):
-        sums = lax.fori_loop(n * step, (n + 1) * step, add, sums, unroll=4)
-        if n < 3:
-            xz[near[n]].wait_recv()
-            relay(near[n])
+    step = slots // rz
+
+    def segment(n, sums):
+        sums = lax.fori_loop(0, step, lambda k, c: add((n - 1) * step + k, c), sums, unroll=2)
+        xz(n).wait_recv()
+        relay(n)
+        return sums
+
+    sums = lax.fori_loop(1, rz, segment, sums)
+    lax.fori_loop((rz - 1) * step, slots, add, sums, unroll=2)
 
     def place(p, top):
         for h in range(rows):
@@ -182,17 +195,17 @@
     def piece(dz, dp):
         return lax.rem(zi + rz - dz, rz) * rp + lax.rem(pi + rp - dp, rp)
 
-    order_in = [(0, 0)] + [(dz, 0) for dz in near]
-    order_in += [(dz, dp) for dz in [0] + near for dp in range(1, rp)]
-    top = jnp.zeros((1, tile), F32)
-    y = jnp.zeros((fl, nodes), F32)
-    for dz, dp in order_in:
-        at = piece(dz, dp)
-        top = place(at, top)
-        if dp:
-            xp[dz, dp].wait_recv()
-        x = xall[dz, dp]
-        y = y + mm(x, ahi[at], NT) + mm(x, alo[at], NT)
+    top = lax.fori_loop(0, rz * rp, place, jnp.zeros((1, tile), F32))
+
+    def terms(dz, y):
+        each(1, rp, lambda dp: xp(dz, dp).wait_recv())
+        for dp in range(rp):
+            at = piece(dz, dp)
+            x = xall[dz, dp]
+            y = y + mm(x, ahi[at], NT) + mm(x, alo[at], NT)
+        return y
+
+    y = lax.fori_loop(0, rz, terms, jnp.zeros((fl, nodes), F32))
 
     mine = pl.ds(pl.multiple_of(col * fl, fl), fl)
     yfull[mine, :] = y
@@ -206,17 +219,19 @@
     ones = jnp.ones((16, nodes), BF16)
     y_ext = jnp.concatenate([y_hi, ones], axis=0)
 
-    z = jnp.zeros((fl, nodes), F32)
-    for d in range(cn):
+    def units(n, z):
+        d = cn - 1 - n
         pre = mm(wall[d], y_ext, TN) + mm(wall[d, :fin, :], y_lo, TN)
         gate = jax.nn.sigmoid(pre)
-        cotangent = grad_hidden[...] if d == 0 else hall[d]
-        grad_pre = cotangent.astype(F32) * gate * (1.0 + pre * (1.0 - gate))
+        grad_pre = hall[d].astype(F32) * gate * (1.0 + pre * (1.0 - gate))
         part_hi, part_lo = split(grad_pre)
-        z = z + mm(wall[d, mine, :], part_hi, NN) + mm(wall[d, mine, :], part_lo, NN)
-        if d == 0:
-            hid_out[...] = (pre * gate).astype(BF16)
-            gp_hi, gp_lo = part_hi, part_lo
+        hid_out[...] = (pre * gate).astype(BF16)
+        gp[0] = part_hi
+        gp[1] = part_lo
+        here = wall[d, mine, :]
+        return z + mm(here, part_hi, NN) + mm(here, part_lo, NN)
+
+    z = lax.fori_loop(0, cn, units, jnp.zeros((fl, nodes), F32))
 
     longest = jnp.max(jnp.sum(z * z, axis=1, keepdims=True), axis=0, keepdims=True)
     bound = jnp.sqrt(longest * jnp.max(top, keepdims=True)) + 1e-16
@@ -227,8 +242,12 @@
     z_hi, z_lo = split(z)
     z_two = jnp.concatenate([z_hi, z_lo], axis=0)
 
-    c1 = {}
-    kept = {}
+    def c1(d, dp):
+        return remote(c1send.at[d, dp], c1recv.at[d, dp], c1_ss.at[d, dp], c1_rs.at[d, dp],
+                      pmate(dp))
+
+    def c2(d):
+        return remote(c2send.at[d], c2recv.at[d], c2_ss.at[d], c2_rs.at[d], zmate(d))
 
     def contribute(d):
         for dp in list(range(1, rp)) + [0]:
@@ -239,48 +258,34 @@
                 kept[d] = c
             else:
                 c1send[d, dp] = encode(c, up)
-                c1[d, dp] = go(remote(c1send.at[d, dp], c1recv.at[d, dp], c1_ss.at[d, dp],
-                                      c1_rs.at[d, dp], pmate(dp)))
+                c1(d, dp).start()
 
     def reduced(d):
         total = kept[d]
         for dp in range(1, rp):
-            c1[d, dp].wait_recv()
-            total = total + decode(c1recv[d, dp], down[dp])
+            c1(d, dp).wait_recv()
+            total = total + decode(c1recv[d, dp], s1recv[dp, :1, :1] * (1.0 / TOP / TOP))
         return total
 
-    c2 = {}
-
-    def pass_on(d):
-        c2send[d] = encode(reduced(d), up2)
-        c2[d] = go(remote(c2send.at[d], c2recv.at[d], c2_ss.at[d], c2_rs.at[d], zmate(d)))
-
     contribute(1)
 
-    gw = mm(y_ext, gp_hi, NT) + mm(y_ext, gp_lo, NT)
+    gw = mm(y_ext, gp[0], NT) + mm(y_ext, gp[1], NT)
     gb = gw[fin:fin + 8]
-    gw = gw[:fin] + mm(y_lo, gp_hi, NT)
+    gw = gw[:fin] + mm(y_lo, gp[0], NT)
     for q in range(rp):
         g1send[q, :fr] = gw[q * fr:(q + 1) * fr]
         g1send[q, fr:] = gb
     g1 = [go(remote(g1send.at[lax.rem(pi + d, rp)], g1recv.at[d], g1_ss.at[d], g1_rs.at[d],
                     pmate(d))) for d in range(1, rp)]
-    contribute(2)
-
-    down = {}
+
     for d in range(1, rp):
         s1[d - 1].wait_recv()
-        down[d] = s1recv[d, :1, :1] * (1.0 / TOP / TOP)
         bound = bound + s1recv[d, :1, :1]
     s2send[...] = jnp.broadcast_to(bound, s2send.shape)
     s2 = [go(remote(s2send, s2recv.at[d], s2_ss.at[d], s2_rs.at[d], zmate(d)))
           for d in range(1, rz)]
     up2 = TOP * TOP / bound
 
-    pass_on(1)
-    for d in range(3, rz):
-        contribute(d)
-        pass_on(d - 1)
     part = g1send[pi]
     for d in range(1, rp):
         g1[d - 1].wait_recv()
@@ -288,7 +293,13 @@
     g2send[...] = part
     g2 = [go(remote(g2send, g2recv.at[d], g2_ss.at[d], g2_rs.at[d], zmate(d)))
           for d in range(1, rz)]
-    contribute(0)
+
+    def onward(d):
+        contribute(lax.rem(d + 1, rz))
+        c2send[d] = encode(reduced(d), up2)
+        c2(d).start()
+
+    each(1, rz, onward)
     for d in range(1, rz):
         g2[d - 1].wait_recv()
         part = part + g2recv[d]
@@ -296,28 +307,34 @@
     g3 = [go(remote(gall.at[pi], gall.at[pi], g3_ss.at[d], g3_rs.at[d], pmate(d)))
           for d in range(1, rp)]
     gb_out[...] = part[fr:fr + 1] * norm
-    pass_on(rz - 1)
     total = reduced(0)
     for c in g3:
         c.wait_recv()
     gw_out[...] = gall[...].reshape(fin, hl) * norm
     for d in range(1, rz):
         s2[d - 1].wait_recv()
-        c2[d].wait_recv()
+        c2(d).wait_recv()
         total = total + decode(c2recv[d], s2recv[d, :1, :1] * (1.0 / TOP / TOP))
     gf_out[...] = total
     for c in sent:
         c.wait_send()
 
+    def all_sent(d):
+        each(1, rp, lambda dp: xp(d, dp).wait_send())
+        each(1, rp, lambda dp: c1(d, dp).wait_send())
+
+    def all_passed(d):
+        xz(d).wait_send()
+        c2(d).wait_send()
+
+    each(0, rz, all_sent)
+    each(1, rz, all_passed)
+
 
 def hand_over(*refs):
-    sems = refs[-1]
     half = len(refs) // 2
-    copies = [pltpu.make_async_copy(refs[n], refs[half + n], sems.at[n]) for n in range(half)]
-    for c in copies:
-        c.start()
-    for c in copies:
-        c.wait()
+    for source, target in zip(refs[:half], refs[half:]):
+        target[...] = source[...]
 
 
 def per_device(r, cn, features, order, weight, bias, tiles, coords, counts, grad_hidden):
@@ -356,6 +373,8 @@
             pltpu.VMEM((fin, nodes), F32),
             pltpu.VMEM((cn, fin + 16, hl), BF16),
             pltpu.VMEM((cn, hl, nodes), BF16),
+            pltpu.VMEM((2, hl, nodes), BF16),
+            pltpu.VMEM((rz, fl, nodes), F32),
             pltpu.VMEM((rz, rp, fl, nodes), WIRE),
             pltpu.VMEM((rz, rp, fl, nodes), WIRE),
             pltpu.VMEM((rz, fl, nodes), WIRE),
@@ -390,9 +409,8 @@
     hidden, gf, gw, gb = pl.pallas_call(
         hand_over,
         out_shape=outs,
-        in_specs=[anyw] * 4,
-        out_specs=(anyw,) * 4,
-        scratch_shapes=[dma((4,))],
+        in_specs=[vmem] * 4,
+        out_specs=(vmem,) * 4,
         name="hand_over",
     )(hidden, gf, gw, gb)
     return hidden, gf, gw, gb.reshape(hl)

time: 41.7 us -> 35.5 us (0.85)
  Pallas kernels: 40.9 us -> 34.7 us
    pallas_call x1, Pallas kernels: 7.11 us -> 1.59 us  [per_device(): pl.pallas_call(hand_over, out_shape=outs, in_specs=[vmem] * 4, out_specs=...]
    pallas_call x1, Pallas kernels: 33.8 us -> 33.1 us  [per_device(): pl.pallas_call(functools.partial(layer_kernel, rz, rp, cn, norm), out_sha...]
where the time goes in v5:
time: 35.5 us; the launch traced here: 35.3 us
  Pallas kernels  34.7 us (98%)
  between operations  0.64 us (2%)
    pallas_call x1, Pallas kernels, per_device(): pl.pallas_call(functools.partial(layer_kernel, rz, rp, cn, norm), out_sha...  33.1 us
    pallas_call x1, Pallas kernels, per_device(): pl.pallas_call(hand_over, out_shape=outs, in_specs=[vmem] * 4, out_specs=...  1.59 us

profile of v5, /device:TPU:0, one launch (start us, length us, event | category | flops | bytes accessed | tf_op | source)
XLA Modules:
  0.0 35.3 jit_solution(8589144479730536198)
XLA Ops:
  0.6 33.1 %layer.1 = (bf16[128,256]{1,0:T(8,128)(2,1)}, f32[64,256]{1,0:T(8,128)}, f32[128,128]{1,0:T(8,128)}, f32[1,128]{1,0:T(1,128)}) custom-call(s32[1,256]{1,0:T(1,128)} %bitcast.3, bf16[64,256]{1,0:T(8,128)(2,1)} %feat.1, bf16[128,128]{1,0:T(8,128)(2,1)} %weight.1, bf16[1,128]{1,0:T(2,128)(2,1)} %bitcast.4, bf16[128,256]{1,0:T(8,128)(2,1)} %grad_hidden.1, ...), custom_call_target="tpu_custom_call" | custom-call | tf_op jit(solution)/shard_map/layer/pallas_call | solution.py:360
  33.7 1.6 %hand_over.1 = (bf16[128,256]{1,0:T(8,128)(2,1)}, f32[64,256]{1,0:T(8,128)}, f32[128,128]{1,0:T(8,128)}, f32[1,128]{1,0:T(1,128)}) custom-call(bf16[128,256]{1,0:T(8,128)(2,1)} %get-tuple-element.12.refs_0_, f32[64,256]{1,0:T(8,128)} %get-tuple-element.13.refs_1_, f32[128,128]{1,0:T(8,128)} %get-tuple-element.14.refs_2_, f32[1,128]{1,0:T(1,128)} %get-tuple-element.15.refs_3_), custom_call_target="tpu_custom_call" | custom-call | tf_op jit(solution)/shard_map/hand_over/pallas_call | solution.py:409

commit v6 on v3

--- a/solution.py
+++ b/solution.py
@@ -188,6 +188,7 @@
     for dz in [0] + near:
         for dp in range(1, rp):
             xp[dz, dp].wait_recv()
+        for dp in range(1, rp):
             y = y + term(dz, dp)
 
     mine = pl.ds(pl.multiple_of(col * fl, fl), fl)
@@ -239,21 +240,23 @@
     kept = {}
 
     def contribute(d):
-        for dp in list(range(1, rp)) + [0]:
+        parts = []
+        for dp in range(rp):
             at = lax.rem(zi + d, rz) * rp + lax.rem(pi + dp, rp)
             both = mm(z_two, ahi[at], NN)
-            c = both[:fl] + both[fl:] + mm(z_hi, alo[at], NN)
-            if dp == 0:
-                kept[d] = c
-            else:
-                c1send[d, dp] = encode(c, up)
-                c1[d, dp] = go(remote(c1send.at[d, dp], c1recv.at[d, dp], c1_ss.at[d, dp],
-                                      c1_rs.at[d, dp], pmate(dp)))
+            parts.append(both[:fl] + both[fl:] + mm(z_hi, alo[at], NN))
+        kept[d] = parts[0]
+        for dp in range(1, rp):
+            c1send[d, dp] = encode(parts[dp], up)
+        for dp in range(1, rp):
+            c1[d, dp] = go(remote(c1send.at[d, dp], c1recv.at[d, dp], c1_ss.at[d, dp],
+                                  c1_rs.at[d, dp], pmate(dp)))
 
     def reduced(d):
         total = kept[d]
         for dp in range(1, rp):
             c1[d, dp].wait_recv()
+        for dp in range(1, rp):
             total = total + decode(c1recv[d, dp], down[dp])
         return total
 

time: 34 us -> 34.1 us (level)
  no operation moved by 1% of the time
where the time goes in v6:
time: 34.1 us; the launch traced here: 33.9 us
  Pallas kernels  33.2 us (97%)
  between operations  0.64 us (2%)
    pallas_call x1, Pallas kernels, per_device(): pl.pallas_call(functools.partial(layer_kernel, rz, rp, cn, norm), out_sha...  31.7 us
    pallas_call x1, Pallas kernels, per_device(): pl.pallas_call(hand_over, out_shape=outs, in_specs=[vmem] * 4, out_specs=...  1.59 us

profile of v6, /device:TPU:0, one launch (start us, length us, event | category | flops | bytes accessed | tf_op | source)
XLA Modules:
  0.0 33.9 jit_solution(10510935035218247842)
XLA Ops:
  0.6 31.7 %layer.1 = (bf16[128,256]{1,0:T(8,128)(2,1)}, f32[64,256]{1,0:T(8,128)}, f32[128,128]{1,0:T(8,128)}, f32[1,128]{1,0:T(1,128)}) custom-call(s32[1,256]{1,0:T(1,128)} %bitcast.3, bf16[64,256]{1,0:T(8,128)(2,1)} %feat.1, bf16[128,128]{1,0:T(8,128)(2,1)} %weight.1, bf16[1,128]{1,0:T(2,128)(2,1)} %bitcast.4, bf16[128,256]{1,0:T(8,128)(2,1)} %grad_hidden.1, ...), custom_call_target="tpu_custom_call" | custom-call | tf_op jit(solution)/shard_map/layer/pallas_call | solution.py:341
  32.3 1.6 %hand_over.1 = (bf16[128,256]{1,0:T(8,128)(2,1)}, f32[64,256]{1,0:T(8,128)}, f32[128,128]{1,0:T(8,128)}, f32[1,128]{1,0:T(1,128)}) custom-call(bf16[128,256]{1,0:T(8,128)(2,1)} %get-tuple-element.12.refs_0_, f32[64,256]{1,0:T(8,128)} %get-tuple-element.13.refs_1_, f32[128,128]{1,0:T(8,128)} %get-tuple-element.14.refs_2_, f32[1,128]{1,0:T(1,128)} %get-tuple-element.15.refs_3_), custom_call_target="tpu_custom_call" | custom-call | tf_op jit(solution)/shard_map/hand_over/pallas_call | solution.py:387
